TPU v7x, 768 devices: a whole 4x8x12 slice. The times are simulated.
768 devices in a mesh: freq: 32 (over x, y), rcv: 24 (over z, core).
Axes of the slice: x: 4, y: 8, z: 12, core: 2. Of those that a mesh axis runs over, the one named last changes fastest.
Arguments:
- traces: bfloat16 [64, 3072, 1024], P('freq', 'rcv'), may hold values from -6 to 6
- kern_v: bfloat16 [128, 3072, 12, 128], P('freq', 'rcv'), may hold values from -0.375 to 0.375
- kern_u: bfloat16 [128, 24, 1536, 128], P('freq', 'rcv'), may hold values from -0.15625 to 0.15625
- assign: int32 [128], replicated, may hold values from 0 to 127, each once
- tile_rank: int32 [128, 12, 24], P('freq', None, 'rcv'), may hold values from 4 to 64, as said below
Outputs:
- redatumed: float32 [1536, 64, 1024], P('rcv', 'freq')
Inputs may be any that keep to these rules, and one draw needn't show every extreme that they name: assign holds each of 0 to 127 once. Only the first tile_rank[s, i, j] rank columns of a tile count; some tile has rank exactly 64.
All inputs are finite; a program needn't handle non-finite values.
Results may differ from a plain program's by a relative error of at most 0.0059.
Values may be sent and summed in bfloat16 or wider, within the bound.
A program may use at most 64 MiB of HBM per device.

v0:
```python
import math

import jax
import jax.numpy as jnp
from jax import lax
from jax.sharding import PartitionSpec as P


def spectral_tables(assign, recording_values):
    spectral_bin_numbers = assign + 1
    clock_moments = jnp.arange(recording_values, dtype=jnp.int32)
    rotation_radians = clock_moments[:, None] * spectral_bin_numbers[None, :] % recording_values
    angles = rotation_radians.astype(jnp.float32) * (2.0 * math.pi / recording_values)
    cosine = jnp.cos(angles)
    sine = jnp.sin(angles)
    forward = jnp.concatenate([cosine, -sine], axis=1).astype(jnp.bfloat16)
    inverse_transform = jnp.concatenate([cosine.T, -sine.T], axis=0).astype(jnp.bfloat16)
    return (forward, inverse_transform)


def form_weights(product, ranks, ranked):
    real_w = product[:, 0, :, 0] + product[:, 1, :, 1]
    imag_w = product[:, 0, :, 1] - product[:, 1, :, 0]
    inside = jnp.arange(ranked, dtype=jnp.int32)[None, :, None] < ranks[:, None, None]
    real_w = jnp.where(inside, real_w, 0.0).astype(jnp.bfloat16)
    imag_w = jnp.where(inside, imag_w, 0.0).astype(jnp.bfloat16)
    upper = jnp.stack([real_w, imag_w], axis=2)
    bottom = jnp.stack([-imag_w, real_w], axis=2)
    stacked = jnp.stack([upper, bottom], axis=1)
    return stacked


def on_device(traces, kern_v, kern_u, assign, tile_rank):
    local_shots, rcv_rows, recording_values = traces.shape
    slot_count = assign.shape[0]
    local_slots = kern_v.shape[0]
    emitter_patches = kern_v.shape[2]
    rank_cap = kern_v.shape[3] // 2
    sources = kern_u.shape[2]
    half_tile = rcv_rows // 2
    forward, inverse_transform = spectral_tables(assign, recording_values)
    spectra = jnp.dot(
        traces.reshape(local_shots * rcv_rows, recording_values),
        forward,
        preferred_element_type=jnp.float32,
    ) * (1.0 / math.sqrt(recording_values))
    spectra = spectra.astype(jnp.bfloat16).reshape(local_shots, rcv_rows, 2, slot_count)
    spectra = lax.all_to_all(spectra, "freq", split_axis=3, concat_axis=0, tiled=True)
    shots = spectra.shape[0]
    ranks = tile_rank[:, :, 0]
    v_slots = kern_v.reshape(local_slots, rcv_rows, emitter_patches, 2, rank_cap)
    u_rows = kern_u.reshape(local_slots, sources, 2, rank_cap)
    product = jnp.einsum("sriak,vrbs->siakbv", v_slots, spectra, preferred_element_type=jnp.float32)

    def full_weights(product_one, rank_one):
        return form_weights(product_one, rank_one, rank_cap)

    weights = jax.vmap(full_weights)(product, ranks)
    local_matrix_lines = sources // lax.axis_size("rcv")
    blocks = local_matrix_lines * lax.axis_size("rcv") // half_tile
    u_part = u_rows.reshape(local_slots, blocks, half_tile, 2, rank_cap)
    tile_index = jnp.arange(blocks, dtype=jnp.int32) // 2
    chosen = jnp.take(weights, tile_index, axis=1)
    terms = jnp.einsum("sbhpk,sbpkqv->bhvqs", u_part, chosen, preferred_element_type=jnp.float32)
    summed = lax.psum_scatter(
        terms.reshape(local_matrix_lines * lax.axis_size("rcv"), shots * 2 * local_slots),
        "rcv",
        scatter_dimension=0,
        tiled=True,
    )
    partial_y = summed.astype(jnp.bfloat16).reshape(local_matrix_lines, shots, 2, local_slots)
    partial_y = lax.all_to_all(partial_y, "freq", split_axis=1, concat_axis=3, tiled=True)
    out_shots = partial_y.shape[1]
    flattened = partial_y.reshape(local_matrix_lines * out_shots, 2 * slot_count)
    result = jnp.dot(flattened, inverse_transform, preferred_element_type=jnp.float32) * (
        2.0 / math.sqrt(recording_values)
    )
    return result.reshape(local_matrix_lines, out_shots, recording_values)


def solution(mesh):
    placed = (
        P("freq", "rcv", None),
        P("freq", "rcv", None, None),
        P("freq", "rcv", None, None),
        P(),
        P("freq", None, "rcv"),
    )
    return jax.shard_map(
        on_device, mesh=mesh, in_specs=placed, out_specs=P("rcv", "freq", None), check_vma=False
    )
```

profile of v0, /device:TPU:8, one launch (start us, length us, event | category | flops | bytes accessed | tf_op | source)
XLA Modules:
  0.0 196.9 jit_solution(8964969710589104990)
XLA Ops:
  6.5 0.0 copy-start
  6.5 0.7 broadcast_add_fusion
  7.3 2.2 %cosine_convert_fusion.1 = (bf16[1024,128]{1,0:T(8,128)(2,1)S(1)}, bf16[1024,128]{1,0:T(8,128)(2,1)S(1)}) fusion(s32[128]{0:T(128)S(1)} %broadcast_add_fusion), kind=kLoop, calls=%fused_computation.47 | loop fusion | flops 2228224 | bytes 524800 | tf_op jit(solution)/shard_map/convert.2
  9.5 0.0 copy-done
  9.5 0.4 fusion.16
  9.9 0.7 copy.20
  10.6 13.0 %all-to-all-start = ((bf16[2,128,2,128]{1,0,2,3:T(2,128)(2,1)}), bf16[2,128,2,128]{1,0,2,3:T(2,128)(2,1)S(1)}, u32[]{:S(2)}, u32[]{:S(2)}) async-start(bf16[2,128,2,128]{1,0,2,3:T(2,128)(2,1)} %copy.20), calls=%async_computation | async-start | bytes 262144 | tf_op jit(solution)/shard_map/all_to_all | solution.py:48
  23.6 0.0 reduce-scatter.4.cloned.1.call-start
  23.7 1.9 copy.22
  25.6 0.0 copy-start.1
  25.7 6.5 %reshape_reshape.3 = bf16[4,24,64,2,64]{4,3,2,1,0:T(2,128)(2,1)} reshape(bf16[4,1,1536,128]{3,2,1,0:T(8,128)(2,1)} %param.7) | data formatting | bytes 3145728 | tf_op jit(solution)/shard_map/reshape;reshape | solution.py:61
  32.1 0.0 copy-done.1
  32.2 0.1 iota_compare_fusion
  32.2 1.2 all-to-all-done
  33.4 0.1 copy.21
  33.5 1.8 convolution_bitcast_fusion
  35.3 0.5 fusion.38
  35.8 0.4 fusion.14
  36.2 0.7 maximum_bitcast_fusion
  36.9 2.4 %pad_maximum_fusion = bf16[4,12,2,64,2,64]{3,5,1,0,4,2:T(8,128)(2,1)} fusion(bf16[4,12,1,64,2,64]{3,5,1,0,4,2:T(8,128)(2,1)S(1)} %get-tuple-element.8, bf16[4,12,1,64,2,64]{3,5,1,0,4,2:T(8,128)(2,1)S(1)} %get-tuple-element.7), kind=kLoop, calls=%fused_computation.4 | loop fusion | flops 786432 | bytes 3145728 | tf_op jit(solution)/shard_map/vmap()/stack | solution.py:29
  39.3 6.3 %gather_fusion = bf16[24,4,2,64,2,64]{3,5,1,4,2,0:T(8,128)(2,1)} fusion(bf16[4,12,2,64,2,64]{3,5,1,0,4,2:T(8,128)(2,1)} %pad_maximum_fusion, s32[1024]{0:T(1024)S(1)} %pad_clamp_fusion), kind=kCustom, calls=%fused_computation | custom fusion | bytes 6291552 | tf_op jit(solution)/shard_map/jit(_take)/gather | solution.py:63
  45.6 5.5 %fusion.3 = f32[24,64,64,2,4]{1,2,3,4,0:T(8,128)S(1)} fusion(bf16[4,24,64,2,64,1]{4,3,2,1,0,5:T(2,128)(2,1)} %bitcast.85, bf16[24,4,2,64,2,64]{3,5,1,4,2,0:T(8,128)(2,1)} %gather_fusion, pred[24]{0:T(512)(128)(4,1)S(1)} %compare_and_fusion), kind=kOutput, calls=%fused_computation.6 | convolution fusion | flops 202899456 | bytes 7864344 | tf_op jit(solution)/shard_map/sbhpk,sbpkqv->bhvqs/dot_general | solution.py:64
  51.2 6.3 %copy.27 = f32[24,64,64,2,4]{1,0,4,3,2:T(8,128)} copy(f32[24,64,64,2,4]{1,2,3,4,0:T(8,128)S(1)} %fusion.3) | data formatting | bytes 6291456 | tf_op jit(solution)/shard_map/sbhpk,sbpkqv->bhvqs/transpose | solution.py:64
  57.5 6.2 %reshape.141 = f32[1536,512]{0,1:T(8,128)} reshape(f32[24,64,64,2,4]{1,0,4,3,2:T(8,128)} %copy.27) | data formatting | bytes 6291456 | tf_op jit(solution)/shard_map/reshape | solution.py:66
  63.6 3.5 %copy.35 = f32[1536,512]{1,0:T(8,128)} copy(f32[1536,512]{0,1:T(8,128)} %reshape.141) | data formatting | bytes 6291456
  67.2 0.0 reduce-scatter.4.cloned.1.call-update
  67.2 93.0 %reduce-scatter.4.cloned.1.call-done = f32[64,512]{1,0:T(8,128)} async-done(((f32[1536,512]{1,0:T(8,128)}), f32[64,512]{1,0:T(8,128)}) %reduce-scatter.4.cloned.1.call-update) | async-done | bytes 131088
  160.2 1.0 copy.36
  161.2 0.8 reshape.159
  162.0 9.8 %all-to-all-start.1 = ((bf16[32,2,512]{2,1,0:T(2,128)(2,1)}), bf16[32,2,512]{2,1,0:T(2,128)(2,1)S(1)}, u32[]{:S(2)}, u32[]{:S(2)}) async-start(bf16[32,2,512]{2,1,0:T(2,128)(2,1)} %reshape.159), calls=%async_computation.1 | async-start | bytes 131072 | tf_op jit(solution)/shard_map/all_to_all | solution.py:72
  171.8 2.4 %cosine_convert_fusion = (bf16[128,1024]{1,0:T(8,128)(2,1)S(1)}, bf16[128,1024]{1,0:T(8,128)(2,1)S(1)}) fusion(s32[128]{0:T(128)S(1)} %broadcast_add_fusion), kind=kLoop, calls=%fused_computation.43 | loop fusion | flops 2228224 | bytes 524800 | tf_op jit(solution)/shard_map/convert
  174.2 6.6 %all-to-all-done.1 = bf16[32,2,512]{2,1,0:T(2,128)(2,1)S(1)} async-done(((bf16[32,2,512]{2,1,0:T(2,128)(2,1)}), bf16[32,2,512]{2,1,0:T(2,128)(2,1)S(1)}, u32[]{:S(2)}, u32[]{:S(2)}) %all-to-all-start.1) | async-done | bytes 65568 | tf_op jit(solution)/shard_map/all_to_all | solution.py:72
  180.9 0.1 reshape.160
  181.0 3.7 %copy.28 = bf16[64,32,2,2,4]{4,1,3,2,0:T(8,128)(2,1)S(1)} copy(bf16[64,32,2,2,4]{0,4,3,2,1:T(4,128)(2,1)S(1)} %bitcast.87) | data formatting | bytes 131072 | tf_op jit(solution)/shard_map/all_to_all | solution.py:72
  184.7 4.0 %reshape.143 = bf16[128,256]{1,0:T(8,128)(2,1)S(1)} reshape(bf16[64,2,2,32,4]{4,3,2,1,0:T(8,128)(2,1)S(1)} %bitcast.83) | data formatting | bytes 131072 | tf_op jit(solution)/shard_map/reshape | solution.py:74
  188.7 0.2 convolution_multiply_fusion
  189.0 1.1 reshape.144
  (4 shorter events, 0.1 us)
Async XLA Ops:
  6.5 2.9 %copy-start = (bf16[2,128,1024]{2,1,0:T(8,128)(2,1)S(1)}, bf16[2,128,1024]{2,1,0:T(8,128)(2,1)}, u32[]{:S(2)}) copy-start(bf16[2,128,1024]{2,1,0:T(8,128)(2,1)} %param.5) | copy-start | bytes 1572868
  10.6 22.8 %all-to-all-start = ((bf16[2,128,2,128]{1,0,2,3:T(2,128)(2,1)}), bf16[2,128,2,128]{1,0,2,3:T(2,128)(2,1)S(1)}, u32[]{:S(2)}, u32[]{:S(2)}) async-start(bf16[2,128,2,128]{1,0,2,3:T(2,128)(2,1)} %copy.20), calls=%async_computation | async-start | bytes 262144 | tf_op jit(solution)/shard_map/all_to_all | solution.py:48
  23.6 136.5 %reduce-scatter.4.cloned.1.call-start = ((), (), s32[]{:S(2)}) async-start(), calls=%async_computation.3 | async-start | bytes 3276800
  25.6 6.5 %copy-start.1 = (s32[4,12,1]{1,2,0:T(1,128)S(1)}, s32[4,12,1]{1,2,0:T(1,128)}, u32[]{:S(2)}) copy-start(s32[4,12,1]{1,2,0:T(1,128)} %param.9) | copy-start | bytes 580
  162.0 18.9 %all-to-all-start.1 = ((bf16[32,2,512]{2,1,0:T(2,128)(2,1)}), bf16[32,2,512]{2,1,0:T(2,128)(2,1)S(1)}, u32[]{:S(2)}, u32[]{:S(2)}) async-start(bf16[32,2,512]{2,1,0:T(2,128)(2,1)} %reshape.159), calls=%async_computation.1 | async-start | bytes 131072 | tf_op jit(solution)/shard_map/all_to_all | solution.py:72
Sparse Core Ops, SparseCore 0:
  67.3 92.8 reduce-scatter.3
where the time goes:
time: 197 us
  waiting for transfers between devices  101 us (51%)
  local copies, waits for them, and re-layouts  42.4 us (22%)
  starting transfers between devices  22.8 us (12%)
  between operations  13.6 us (7%)
  other arithmetic  9.42 us (5%)
  matrix products  7.93 us (4%)
    unnamed x2, waiting for transfers between devices  93 us
    all_to_all x1, starting transfers between devices, on_device(): lax.all_to_all(spectra, 'freq', split_axis=3, concat_axis=0, tiled=True)  13 us
    all_to_all x1, starting transfers between devices, on_device(): lax.all_to_all(partial_y, 'freq', split_axis=1, concat_axis=3, tiled=True)  9.83 us
    unnamed x9, local copies, waits for them, and re-layouts  7.37 us
    all_to_all x1, waiting for transfers between devices, on_device(): lax.all_to_all(partial_y, 'freq', split_axis=1, concat_axis=3, tiled=True)  6.65 us
    another operation x1, local copies, waits for them, and re-layouts, on_device(): u_part = u_rows.reshape(local_slots, blocks, half_tile, 2, rank_cap)  6.5 us
    gather x1, local copies, waits for them, and re-layouts, on_device(): chosen = jnp.take(weights, tile_index, axis=1)  6.34 us
    transpose x1, local copies, waits for them, and re-layouts, on_device(): jnp.einsum('sbhpk,sbpkqv->bhvqs', u_part, chosen, preferred_element_type=...  6.31 us
  transfers between devices with their start and end apart: 3, of which 3 were waited for; matrix products, arithmetic and copies ran while one was open for 6% of the time, Pallas kernels for 0%

commit v1 on v0

v1 whole, which is shorter than its diff:
```python
import functools
import math

import jax
import jax.numpy as jnp
import ml_dtypes
import numpy as np
from jax import lax
from jax.experimental import pallas as pl
from jax.experimental.pallas import tpu as pltpu
from jax.sharding import PartitionSpec as P

MESH = pl.DeviceIdType.MESH
F32 = jnp.float32
BF16 = jnp.bfloat16
NT = (((1,), (1,)), ((), ()))
NN = (((1,), (0,)), ((), ()))
TN = (((0,), (0,)), ((), ()))


def dot(a, b, dims):
    return lax.dot_general(a, b, dims, preferred_element_type=F32)


def bin_table(bins, moments):
    clock = np.arange(moments)[None, :]
    turns = (np.arange(bins)[:, None] + 1) * clock % moments
    angles = (turns.astype(np.float32) * np.float32(2.0 * math.pi / moments)).astype(np.float64)
    return np.concatenate([np.cos(angles), -np.sin(angles)], axis=0).astype(ml_dtypes.bfloat16)


def shot_order(groups, slots, shots):
    local = shots // groups
    rows = np.arange(groups * 2 * slots)
    lanes = np.arange(slots * 2 * shots)
    group, part, slot = rows // (2 * slots), rows // slots % 2, rows % slots
    lane_slot, lane_part, lane_shot = lanes // (2 * shots), lanes // shots % 2, lanes % shots
    same = (
        (group[:, None] == lane_shot[None, :] // local)
        & (part[:, None] == lane_part[None, :])
        & (slot[:, None] == lane_slot[None, :])
    )
    return same.astype(ml_dtypes.bfloat16)


def kernel(
    nf,
    nr,
    pieces,
    traces_hbm,
    v_hbm,
    u_hbm,
    table_hbm,
    order_hbm,
    assign_ref,
    rank_ref,
    out_ref,
    traces,
    v_raw,
    v_both,
    u_all,
    table,
    order,
    slot_table,
    x_send,
    x_recv,
    x_wide,
    left,
    y_own,
    pair_send,
    pair_recv,
    ring_send,
    ring_recv,
    y_send,
    y_recv,
    load_sem,
    x_sem,
    y_sem,
    pair_send_sem,
    pair_recv_sem,
    ring_send_sem,
    ring_recv_sem,
):
    slots, tiles, rows, cols = v_raw.shape
    half = rows // 2
    rank_cap = cols // 2
    bins = table.shape[0] // 2
    shots = left.shape[1] // 2
    nz = nr // 2
    steps = nz // 2
    wide = slots * cols
    width = wide // pieces
    f = lax.axis_index("freq")
    r = lax.axis_index("rcv")
    z = r // 2
    c = r % 2
    partner = r + 1 - 2 * c
    below = lax.rem(r + nr - 2, nr)
    above = lax.rem(r + 2, nr)

    loads = [
        pltpu.make_async_copy(traces_hbm, traces, load_sem.at[0]),
        pltpu.make_async_copy(table_hbm, table, load_sem.at[1]),
        pltpu.make_async_copy(v_hbm, v_raw, load_sem.at[2]),
        pltpu.make_async_copy(order_hbm, order, load_sem.at[3]),
    ]
    for s in range(slots):
        loads.append(
            pltpu.make_async_copy(u_hbm.at[s], u_all.at[:, pl.ds(s * cols, cols)], load_sem.at[4 + s])
        )
    for load in loads:
        load.start()

    barrier = pltpu.get_barrier_semaphore()

    def greet(i, carry):
        p = lax.rem(f + i, nf)
        pl.semaphore_signal(barrier, inc=1, device_id=(p, r), device_id_type=MESH)
        return carry

    lax.fori_loop(1, nf, greet, 0)
    for other in (partner, below, above):
        pl.semaphore_signal(barrier, inc=1, device_id=(f, other), device_id_type=MESH)

    n2 = 2 * bins
    row = lax.broadcasted_iota(jnp.int32, (n2, bins), 0)
    lane = lax.broadcasted_iota(jnp.int32, (n2, bins), 1)
    slot_of = row // (2 * slots) * slots + row % slots
    held = jnp.where(lane == slot_of, assign_ref[...].astype(F32), 0.0)
    held = jnp.sum(held, axis=1, keepdims=True)
    part_of = lax.broadcasted_iota(jnp.int32, (n2, 1), 0) // slots % 2
    want = held + (part_of * bins).astype(F32)
    lanes = lax.broadcasted_iota(jnp.int32, (n2, n2), 1).astype(F32)
    permute = jnp.where(lanes == want, 1.0, 0.0).astype(BF16)

    loads[0].wait()
    loads[1].wait()
    spectra = dot(table[...], traces[...], NT) * (1.0 / math.sqrt(table.shape[1]))
    spectra = dot(permute, spectra.astype(BF16), NN)
    groups = [spectra[:, k * rows : (k + 1) * rows].reshape(nf, 2 * slots, rows) for k in range(2)]
    block = 4 * slots
    x_send[...] = jnp.concatenate(groups, axis=1).reshape(nf * block, rows).astype(BF16)
    mine = pl.ds(pl.multiple_of(f * block, block), block)
    x_recv[mine, :] = x_send[mine, :]

    pl.semaphore_wait(barrier, nf + 2)

    def send_x(i, carry):
        p = lax.rem(f + i, nf)
        pltpu.make_async_remote_copy(
            src_ref=x_send.at[pl.ds(pl.multiple_of(p * block, block), block), :],
            dst_ref=x_recv.at[mine, :],
            send_sem=x_sem.at[0],
            recv_sem=x_sem.at[1],
            device_id=(p, r),
            device_id_type=MESH,
        ).start()
        return carry

    lax.fori_loop(1, nf, send_x, 0)

    loads[2].wait()
    lane_v = lax.broadcasted_iota(jnp.int32, (rows, cols), 1)
    lane_k = lane_v % rank_cap
    upper = lane_v < rank_cap

    for s in range(slots):

        def prepare(i, carry, s=s):
            v = jnp.where(lane_k < rank_ref[s, i], v_raw[s, i].astype(F32), 0.0)
            turned = pltpu.roll(v, rank_cap, 1)
            v_both[s, i, :rows, :] = v.astype(BF16)
            v_both[s, i, rows:, :] = jnp.where(upper, turned, -turned).astype(BF16)
            return carry

        lax.fori_loop(0, tiles, prepare, 0)
    slot_table[...] = dot(permute, table[...], NN).astype(BF16)
    for load in loads[3:]:
        load.wait()

    all_x = pltpu.make_async_remote_copy(
        src_ref=x_send.at[pl.ds(0, (nf - 1) * block), :],
        dst_ref=x_recv.at[pl.ds(0, (nf - 1) * block), :],
        send_sem=x_sem.at[0],
        recv_sem=x_sem.at[1],
        device_id=(f, partner),
        device_id_type=MESH,
    )
    all_x.wait_recv()
    x_wide[...] = x_recv[...].astype(F32)
    for s in range(slots):
        real = x_wide[pl.ds(s, shots, stride=2 * slots), :].astype(BF16)
        imag = x_wide[pl.ds(slots + s, shots, stride=2 * slots), :].astype(BF16)
        left[s, :shots, :rows] = real
        left[s, :shots, rows:] = imag
        left[s, shots:, :rows] = imag
        left[s, shots:, rows:] = -real

    def tile_at(n):
        if n == 0:
            return lax.rem(z + steps, nz)
        if n == nz - 1:
            return z
        k = (n + 1) // 2
        return lax.rem(z + steps + k, nz) if n % 2 else lax.rem(z + steps + nz - k, nz)

    def pair_copy(n):
        return pltpu.make_async_remote_copy(
            src_ref=pair_send.at[n],
            dst_ref=pair_recv.at[n],
            send_sem=pair_send_sem.at[n],
            recv_sem=pair_recv_sem.at[n],
            device_id=(f, partner),
            device_id_type=MESH,
        )

    def compute(n):
        i = tile_at(n)
        keep = pl.ds(pl.multiple_of(i * rows + c * half, half), half)
        give = pl.ds(pl.multiple_of(i * rows + (1 - c) * half, half), half)
        for s in range(slots):
            w = dot(left[s], v_both[s, i], NN).astype(BF16)
            at = slice(s * cols, (s + 1) * cols)
            u = jnp.concatenate([u_all[keep, at], u_all[give, at]], axis=0)
            y = dot(u, w, NT)
            y_own[n, :, at] = y[:half]
            pair_send[n, :, at] = y[half:].astype(BF16)
        pair_copy(n).start()

    def ring_copy(way, k, p):
        return pltpu.make_async_remote_copy(
            src_ref=ring_send.at[way, k, p],
            dst_ref=ring_recv.at[way, k, p],
            send_sem=ring_send_sem.at[way, k, p],
            recv_sem=ring_recv_sem.at[way, k, p],
            device_id=(f, above if way else below),
            device_id_type=MESH,
        )

    def first_step(way):
        return range(pieces // 2, pieces) if way else range(pieces // 2)

    def ring_step(k):
        for n in (0,) if k == 0 else (2 * k - 1, 2 * k):
            pair_copy(n).wait_recv()
        for p in range(pieces):
            at = slice(p * width, (p + 1) * width)
            for way in range(2):
                if k == 0 and p not in first_step(way):
                    continue
                n = 0 if k == 0 else 2 * k - 1 + way
                total = y_own[n, :, at] + pair_recv[n, :, at].astype(F32)
                if k >= 2 or (k == 1 and p in first_step(way)):
                    ring_copy(way, k - 1, p).wait_recv()
                    total = total + ring_recv[way, k - 1, p].astype(F32)
                ring_send[way, k, p] = total.astype(BF16)
                ring_copy(way, k, p).start()

    compute(0)
    compute(1)
    compute(2)
    for k in range(steps):
        ring_step(k)
        if k + 2 < steps:
            compute(2 * k + 3)
            compute(2 * k + 4)
        elif k + 2 == steps:
            compute(nz - 1)
    n = nz - 1
    pair_copy(n).wait_recv()
    sums = []
    for p in range(pieces):
        at = slice(p * width, (p + 1) * width)
        total = y_own[n, :, at] + pair_recv[n, :, at].astype(F32)
        for way in range(2):
            ring_copy(way, steps - 1, p).wait_recv()
            total = total + ring_recv[way, steps - 1, p].astype(F32)
        sums.append(total)
    response = jnp.concatenate(sums, axis=1)

    even = lax.broadcasted_iota(jnp.int32, (half, wide), 1) % 2 == 0
    stacked = jnp.concatenate(
        [jnp.where(even, response, 0.0).astype(BF16), jnp.where(even, 0.0, response).astype(BF16)], axis=0
    )
    y_send[...] = dot(order[...], stacked, NT)
    eight = 2 * slots
    mine_y = pl.ds(pl.multiple_of(f * eight, eight), eight)
    y_recv[mine_y, :] = y_send[mine_y, :]

    def send_y(i, carry):
        p = lax.rem(f + i, nf)
        pltpu.make_async_remote_copy(
            src_ref=y_send.at[pl.ds(pl.multiple_of(p * eight, eight), eight), :],
            dst_ref=y_recv.at[mine_y, :],
            send_sem=y_sem.at[0],
            recv_sem=y_sem.at[1],
            device_id=(p, r),
            device_id_type=MESH,
        ).start()
        return carry

    lax.fori_loop(1, nf, send_y, 0)
    all_y = pltpu.make_async_remote_copy(
        src_ref=y_send.at[pl.ds(0, (nf - 1) * eight), :],
        dst_ref=y_recv.at[pl.ds(0, (nf - 1) * eight), :],
        send_sem=y_sem.at[0],
        recv_sem=y_sem.at[1],
        device_id=(f, partner),
        device_id_type=MESH,
    )

    all_x.wait_send()
    for n in range(nz):
        pair_copy(n).wait_send()
    for k in range(steps):
        for way in range(2):
            for p in range(pieces):
                if k or p in first_step(way):
                    ring_copy(way, k, p).wait_send()
    all_y.wait_recv()
    result = dot(y_recv[...].astype(BF16), slot_table[...], TN) * (2.0 / math.sqrt(table.shape[1]))
    out_ref[:, 0, :] = result[:half]
    out_ref[:, 1, :] = result[half:]
    all_y.wait_send()


def on_device(nf, nr, traces, kern_v, kern_u, assign, tile_rank):
    local_shots, rows, moments = traces.shape
    slots, _, tiles, cols = kern_v.shape
    sources = kern_u.shape[2]
    bins = assign.shape[0]
    shots = local_shots * nf
    half = rows // 2
    nz = nr // 2
    steps = nz // 2
    pieces = 2
    wide = slots * cols
    table = jnp.asarray(bin_table(bins, moments))
    order = jnp.asarray(shot_order(nf, slots, shots))
    hbm = pl.BlockSpec(memory_space=pl.ANY)
    vmem = pl.BlockSpec(memory_space=pltpu.VMEM)
    return pl.pallas_call(
        functools.partial(kernel, nf, nr, pieces),
        out_shape=jax.ShapeDtypeStruct((half, local_shots, moments), F32),
        in_specs=[hbm] * 5 + [vmem, pl.BlockSpec(memory_space=pltpu.SMEM)],
        out_specs=vmem,
        scratch_shapes=[
            pltpu.VMEM((local_shots * rows, moments), BF16),
            pltpu.VMEM((slots, tiles, rows, cols), BF16),
            pltpu.VMEM((slots, tiles, 2 * rows, cols), BF16),
            pltpu.VMEM((sources, wide), BF16),
            pltpu.VMEM((2 * bins, moments), BF16),
            pltpu.VMEM((nf * 2 * slots, wide), BF16),
            pltpu.VMEM((2 * bins, moments), BF16),
            pltpu.VMEM((nf * 4 * slots, rows), BF16),
            pltpu.VMEM((nf * 4 * slots, rows), BF16),
            pltpu.VMEM((nf * 4 * slots, rows), F32),
            pltpu.VMEM((slots, 2 * shots, 2 * rows), BF16),
            pltpu.VMEM((nz, half, wide), F32),
            pltpu.VMEM((nz, half, wide), BF16),
            pltpu.VMEM((nz, half, wide), BF16),
            pltpu.VMEM((2, steps, pieces, half, wide // pieces), BF16),
            pltpu.VMEM((2, steps, pieces, half, wide // pieces), BF16),
            pltpu.VMEM((nf * 2 * slots, 2 * half), F32),
            pltpu.VMEM((nf * 2 * slots, 2 * half), F32),
            pltpu.SemaphoreType.DMA((4 + slots,)),
            pltpu.SemaphoreType.DMA((2,)),
            pltpu.SemaphoreType.DMA((2,)),
            pltpu.SemaphoreType.DMA((nz,)),
            pltpu.SemaphoreType.DMA((nz,)),
            pltpu.SemaphoreType.DMA((2, steps, pieces)),
            pltpu.SemaphoreType.DMA((2, steps, pieces)),
        ],
        compiler_params=pltpu.CompilerParams(
            collective_id=0, has_side_effects=True, vmem_limit_bytes=48 * 1024 * 1024
        ),
        name="redatum",
    )(
        traces.reshape(local_shots * rows, moments),
        jnp.transpose(kern_v, (0, 2, 1, 3)),
        kern_u.reshape(slots, sources, cols),
        table,
        order,
        assign.reshape(1, bins),
        tile_rank.reshape(slots, tiles),
    )


def solution(mesh):
    placed = (
        P("freq", "rcv", None),
        P("freq", "rcv", None, None),
        P("freq", "rcv", None, None),
        P(),
        P("freq", None, "rcv"),
    )
    return jax.shard_map(
        functools.partial(on_device, mesh.shape["freq"], mesh.shape["rcv"]),
        mesh=mesh,
        in_specs=placed,
        out_specs=P("rcv", "freq", None),
        check_vma=False,
    )
```

time: 197 us -> 64.3 us (0.33)
  the two profiles are of different devices: /device:TPU:8 before, /device:TPU:2 now
where the time goes in v1:
time: 64.3 us; the launch traced here: 63.9 us
  Pallas kernels  55.9 us (87%)
  local copies, waits for them, and re-layouts  7.98 us (12%)
    pallas_call x1, Pallas kernels, on_device(): pl.pallas_call(functools.partial(kernel, nf, nr, pieces), out_shape=jax.S...  55.9 us
    unnamed x15, local copies, waits for them, and re-layouts  7.98 us

profile of v1, /device:TPU:2, one launch (start us, length us, event | category | flops | bytes accessed | tf_op | source)
XLA Modules:
  0.0 63.9 jit_solution(10290284351693027389)
XLA Ops:
  0.0 0.0 copy-start
  0.0 1.4 %copy-done = bf16[4,128,12,128]{3,1,2,0:T(8,128)(2,1)S(1)} copy-done((bf16[4,128,12,128]{3,1,2,0:T(8,128)(2,1)S(1)}, bf16[4,128,12,128]{3,1,2,0:T(8,128)(2,1)}, u32[]{:S(2)}) %copy-start) | copy-done | bytes 1572888
  1.4 0.0 copy-start.1
  1.4 1.4 %copy-done.1 = bf16[4,1,1536,128]{3,2,1,0:T(8,128)(2,1)S(1)} copy-done((bf16[4,1,1536,128]{3,2,1,0:T(8,128)(2,1)S(1)}, bf16[4,1,1536,128]{3,2,1,0:T(8,128)(2,1)}, u32[]{:S(2)}) %copy-start.1) | copy-done | bytes 1572888
  2.8 0.0 copy-start.2
  2.8 1.0 %copy-done.2 = bf16[2,128,1024]{2,1,0:T(8,128)(2,1)S(1)} copy-done((bf16[2,128,1024]{2,1,0:T(8,128)(2,1)S(1)}, bf16[2,128,1024]{2,1,0:T(8,128)(2,1)}, u32[]{:S(2)}) %copy-start.2) | copy-done | bytes 524312
  3.9 0.0 copy-start.3
  3.9 1.0 %copy-done.3 = bf16[256,1024]{1,0:T(8,128)(2,1)S(1)} copy-done((bf16[256,1024]{1,0:T(8,128)(2,1)S(1)}, bf16[256,1024]{1,0:T(8,128)(2,1)}, u32[]{:S(2)}) %copy-start.3) | copy-done | bytes 524312
  4.9 0.0 copy-start.4
  4.9 0.9 %copy-done.4 = bf16[256,512]{1,0:T(8,128)(2,1)S(1)} copy-done((bf16[256,512]{1,0:T(8,128)(2,1)S(1)}, bf16[256,512]{1,0:T(8,128)(2,1)}, u32[]{:S(2)}) %copy-start.4) | copy-done | bytes 262168
  5.9 0.0 copy-start.5
  5.9 0.7 %copy-done.5 = s32[4,12,1]{1,2,0:T(1,128)S(1)} copy-done((s32[4,12,1]{1,2,0:T(1,128)S(1)}, s32[4,12,1]{1,2,0:T(1,128)}, u32[]{:S(2)}) %copy-start.5) | copy-done | bytes 216
  6.5 0.0 copy-start.6
  6.5 0.7 %copy-done.6 = s32[128]{0:T(128)S(1)} copy-done((s32[128]{0:T(128)S(1)}, s32[128]{0:T(128)}, u32[]{:S(2)}) %copy-start.6) | copy-done | bytes 536
  7.2 55.9 %redatum.1 = f32[64,2,1024]{2,1,0:T(2,128)S(1)} custom-call(bf16[256,1024]{1,0:T(8,128)(2,1)S(1)} %bitcast.7, bf16[4,12,128,128]{3,2,1,0:T(8,128)(2,1)S(1)} %bitcast.5, bf16[4,1536,128]{2,1,0:T(8,128)(2,1)S(1)} %bitcast.6, bf16[256,1024]{1,0:T(8,128)(2,1)S(1)} %copy-done.3, bf16[256,512]{1,0:T(8,128)(2,1)S(1)} %copy-done.4, s32[1,128]{1,0:T(1,128)S(1)} %bitcast.9, ...), custom_call_target="tpu_custom_call" | custom-call | tf_op jit(solution)/shard_map/redatum/pallas_call | solution.py:342
  63.1 0.8 %copy.9 = f32[64,2,1024]{2,1,0:T(2,128)} copy(f32[64,2,1024]{2,1,0:T(2,128)S(1)} %redatum.1) | data formatting | bytes 1048576
Async XLA Ops:
  0.0 1.4 %copy-start = (bf16[4,128,12,128]{3,1,2,0:T(8,128)(2,1)S(1)}, bf16[4,128,12,128]{3,1,2,0:T(8,128)(2,1)}, u32[]{:S(2)}) copy-start(bf16[4,128,12,128]{3,1,2,0:T(8,128)(2,1)} %param.8) | copy-start | bytes 4718596
  1.4 1.4 %copy-start.1 = (bf16[4,1,1536,128]{3,2,1,0:T(8,128)(2,1)S(1)}, bf16[4,1,1536,128]{3,2,1,0:T(8,128)(2,1)}, u32[]{:S(2)}) copy-start(bf16[4,1,1536,128]{3,2,1,0:T(8,128)(2,1)} %param.9) | copy-start | bytes 4718596
  2.8 1.0 %copy-start.2 = (bf16[2,128,1024]{2,1,0:T(8,128)(2,1)S(1)}, bf16[2,128,1024]{2,1,0:T(8,128)(2,1)}, u32[]{:S(2)}) copy-start(bf16[2,128,1024]{2,1,0:T(8,128)(2,1)} %param.7) | copy-start | bytes 1572868
  3.9 1.0 %copy-start.3 = (bf16[256,1024]{1,0:T(8,128)(2,1)S(1)}, bf16[256,1024]{1,0:T(8,128)(2,1)}, u32[]{:S(2)}) copy-start(bf16[256,1024]{1,0:T(8,128)(2,1)} %constant.4.clone.table_hbm) | copy-start | bytes 1572868
  4.9 0.9 %copy-start.4 = (bf16[256,512]{1,0:T(8,128)(2,1)S(1)}, bf16[256,512]{1,0:T(8,128)(2,1)}, u32[]{:S(2)}) copy-start(bf16[256,512]{1,0:T(8,128)(2,1)} %constant.5.clone.order_hbm) | copy-start | bytes 786436
  5.9 0.7 %copy-start.5 = (s32[4,12,1]{1,2,0:T(1,128)S(1)}, s32[4,12,1]{1,2,0:T(1,128)}, u32[]{:S(2)}) copy-start(s32[4,12,1]{1,2,0:T(1,128)} %param.11) | copy-start | bytes 580
  6.5 0.7 %copy-start.6 = (s32[128]{0:T(128)S(1)}, s32[128]{0:T(128)}, u32[]{:S(2)}) copy-start(s32[128]{0:T(128)} %param.10) | copy-start | bytes 1540

commit v2 on v1

--- a/solution.py
+++ b/solution.py
@@ -16,10 +16,17 @@
 NT = (((1,), (1,)), ((), ()))
 NN = (((1,), (0,)), ((), ()))
 TN = (((0,), (0,)), ((), ()))
+ACROSS = 4
 
 
 def dot(a, b, dims):
     return lax.dot_general(a, b, dims, preferred_element_type=F32)
+
+
+def far_first(groups):
+    along = groups // ACROSS
+    offsets = [(a, b) for a in range(ACROSS) for b in range(along) if (a, b) != (0, 0)]
+    return sorted(offsets, key=lambda o: -min(o[0], ACROSS - o[0]) - min(o[1], along - o[1]))
 
 
 def bin_table(bins, moments):
@@ -95,8 +102,13 @@
     z = r // 2
     c = r % 2
     partner = r + 1 - 2 * c
-    below = lax.rem(r + nr - 2, nr)
-    above = lax.rem(r + 2, nr)
+    mates = [[lax.rem(r + nr - 2 * hops, nr), lax.rem(r + 2 * hops, nr)] for hops in (1, 2)]
+    peers = far_first(nf)
+
+    def peer(offset):
+        across, along = offset
+        columns = nf // ACROSS
+        return lax.rem(f // columns + across, ACROSS) * columns + lax.rem(f + along, columns)
 
     loads = [
         pltpu.make_async_copy(traces_hbm, traces, load_sem.at[0]),
@@ -119,7 +131,7 @@
         return carry
 
     lax.fori_loop(1, nf, greet, 0)
-    for other in (partner, below, above):
+    for other in [partner] + mates[0] + mates[1]:
         pl.semaphore_signal(barrier, inc=1, device_id=(f, other), device_id_type=MESH)
 
     n2 = 2 * bins
@@ -143,10 +155,10 @@
     mine = pl.ds(pl.multiple_of(f * block, block), block)
     x_recv[mine, :] = x_send[mine, :]
 
-    pl.semaphore_wait(barrier, nf + 2)
-
-    def send_x(i, carry):
-        p = lax.rem(f + i, nf)
+    pl.semaphore_wait(barrier, nf + 4)
+
+    for offset in peers:
+        p = peer(offset)
         pltpu.make_async_remote_copy(
             src_ref=x_send.at[pl.ds(pl.multiple_of(p * block, block), block), :],
             dst_ref=x_recv.at[mine, :],
@@ -155,9 +167,6 @@
             device_id=(p, r),
             device_id_type=MESH,
         ).start()
-        return carry
-
-    lax.fori_loop(1, nf, send_x, 0)
 
     loads[2].wait()
     lane_v = lax.broadcasted_iota(jnp.int32, (rows, cols), 1)
@@ -227,54 +236,69 @@
             pair_send[n, :, at] = y[half:].astype(BF16)
         pair_copy(n).start()
 
-    def ring_copy(way, k, p):
+    def ring_copy(way, m, p):
         return pltpu.make_async_remote_copy(
-            src_ref=ring_send.at[way, k, p],
-            dst_ref=ring_recv.at[way, k, p],
-            send_sem=ring_send_sem.at[way, k, p],
-            recv_sem=ring_recv_sem.at[way, k, p],
-            device_id=(f, above if way else below),
+            src_ref=ring_send.at[way, m, p],
+            dst_ref=ring_recv.at[way, m, p],
+            send_sem=ring_send_sem.at[way, m, p],
+            recv_sem=ring_recv_sem.at[way, m, p],
+            device_id=(f, mates[1 - m % 2][way]),
             device_id_type=MESH,
         )
 
-    def first_step(way):
+    def sent(way, m):
+        if m:
+            return range(pieces)
         return range(pieces // 2, pieces) if way else range(pieces // 2)
 
-    def ring_step(k):
-        for n in (0,) if k == 0 else (2 * k - 1, 2 * k):
+    def own_part(n, p):
+        at = slice(p * width, (p + 1) * width)
+        return y_own[n, :, at] + pair_recv[n, :, at].astype(F32)
+
+    def arrived(way, m, p):
+        ring_copy(way, m, p).wait_recv()
+        return ring_recv[way, m, p].astype(F32)
+
+    def ring_stage(m):
+        for n in (0,) if m == 0 else (2 * m - 1, 2 * m):
             pair_copy(n).wait_recv()
         for p in range(pieces):
-            at = slice(p * width, (p + 1) * width)
             for way in range(2):
-                if k == 0 and p not in first_step(way):
+                if p not in sent(way, m):
                     continue
-                n = 0 if k == 0 else 2 * k - 1 + way
-                total = y_own[n, :, at] + pair_recv[n, :, at].astype(F32)
-                if k >= 2 or (k == 1 and p in first_step(way)):
-                    ring_copy(way, k - 1, p).wait_recv()
-                    total = total + ring_recv[way, k - 1, p].astype(F32)
-                ring_send[way, k, p] = total.astype(BF16)
-                ring_copy(way, k, p).start()
+                total = own_part(0 if m == 0 else 2 * m - 1 + way, p)
+                if m and m % 2 == 0:
+                    for before in (m - 2, m - 1):
+                        if p in sent(way, before):
+                            total = total + arrived(way, before, p)
+                ring_send[way, m, p] = total.astype(BF16)
+                ring_copy(way, m, p).start()
 
     compute(0)
     compute(1)
     compute(2)
-    for k in range(steps):
-        ring_step(k)
-        if k + 2 < steps:
-            compute(2 * k + 3)
-            compute(2 * k + 4)
-        elif k + 2 == steps:
+    ring_stage(0)
+    ring_stage(1)
+    compute(3)
+    compute(4)
+    for m in range(2, steps, 2):
+        compute(2 * m + 1)
+        compute(2 * m + 2)
+        ring_stage(m + 1)
+        if m + 2 < steps:
+            compute(2 * m + 3)
+            compute(2 * m + 4)
+        else:
             compute(nz - 1)
+        ring_stage(m)
     n = nz - 1
     pair_copy(n).wait_recv()
     sums = []
     for p in range(pieces):
-        at = slice(p * width, (p + 1) * width)
-        total = y_own[n, :, at] + pair_recv[n, :, at].astype(F32)
+        total = own_part(n, p)
         for way in range(2):
-            ring_copy(way, steps - 1, p).wait_recv()
-            total = total + ring_recv[way, steps - 1, p].astype(F32)
+            for m in (steps - 2, steps - 1):
+                total = total + arrived(way, m, p)
         sums.append(total)
     response = jnp.concatenate(sums, axis=1)
 
@@ -287,8 +311,8 @@
     mine_y = pl.ds(pl.multiple_of(f * eight, eight), eight)
     y_recv[mine_y, :] = y_send[mine_y, :]
 
-    def send_y(i, carry):
-        p = lax.rem(f + i, nf)
+    for offset in peers:
+        p = peer(offset)
         pltpu.make_async_remote_copy(
             src_ref=y_send.at[pl.ds(pl.multiple_of(p * eight, eight), eight), :],
             dst_ref=y_recv.at[mine_y, :],
@@ -297,9 +321,7 @@
             device_id=(p, r),
             device_id_type=MESH,
         ).start()
-        return carry
-
-    lax.fori_loop(1, nf, send_y, 0)
+
     all_y = pltpu.make_async_remote_copy(
         src_ref=y_send.at[pl.ds(0, (nf - 1) * eight), :],
         dst_ref=y_recv.at[pl.ds(0, (nf - 1) * eight), :],
@@ -315,7 +337,7 @@
     for k in range(steps):
         for way in range(2):
             for p in range(pieces):
-                if k or p in first_step(way):
+                if p in sent(way, k):
                     ring_copy(way, k, p).wait_send()
     all_y.wait_recv()
     result = dot(y_recv[...].astype(BF16), slot_table[...], TN) * (2.0 / math.sqrt(table.shape[1]))
@@ -337,7 +359,7 @@
     wide = slots * cols
     table = jnp.asarray(bin_table(bins, moments))
     order = jnp.asarray(shot_order(nf, slots, shots))
-    hbm = pl.BlockSpec(memory_space=pl.ANY)
+    hbm = pl.BlockSpec(memory_space=pltpu.HBM)
     vmem = pl.BlockSpec(memory_space=pltpu.VMEM)
     return pl.pallas_call(
         functools.partial(kernel, nf, nr, pieces),
@@ -372,7 +394,7 @@
             pltpu.SemaphoreType.DMA((2, steps, pieces)),
         ],
         compiler_params=pltpu.CompilerParams(
-            collective_id=0, has_side_effects=True, vmem_limit_bytes=48 * 1024 * 1024
+            collective_id=0, has_side_effects=True, vmem_limit_bytes=56 * 1024 * 1024
         ),
         name="redatum",
     )(

time: 64.3 us -> 53.3 us (0.83)
  the two profiles are of different devices: /device:TPU:2 before, /device:TPU:8 now
where the time goes in v2:
time: 53.3 us; the launch traced here: 52.9 us
  Pallas kernels  51 us (96%)
  local copies, waits for them, and re-layouts  1.87 us (4%)
    pallas_call x1, Pallas kernels, on_device(): pl.pallas_call(functools.partial(kernel, nf, nr, pieces), out_shape=jax.S...  51 us
    unnamed x1, local copies, waits for them, and re-layouts  1.87 us

profile of v2, /device:TPU:8, one launch (start us, length us, event | category | flops | bytes accessed | tf_op | source)
XLA Modules:
  0.0 52.9 jit_solution(9943853638432435990)
XLA Ops:
  0.0 51.0 %redatum.1 = f32[64,2,1024]{2,1,0:T(2,128)} custom-call(bf16[256,1024]{1,0:T(8,128)(2,1)} %bitcast.7, bf16[4,12,128,128]{3,2,1,0:T(8,128)(2,1)} %bitcast.5, bf16[4,1536,128]{2,1,0:T(8,128)(2,1)} %bitcast.6, bf16[256,1024]{1,0:T(8,128)(2,1)} %constant.4.clone.table_hbm, bf16[256,512]{1,0:T(8,128)(2,1)} %constant.5.clone.order_hbm, s32[1,128]{1,0:T(1,128)} %bitcast.9, ...), custom_call_target="tpu_custom_call" | custom-call | tf_op jit(solution)/shard_map/redatum/pallas_call | solution.py:364
  51.1 1.9 %copy.9 = f32[64,2,1024]{2,1,0:T(2,128)} copy(f32[64,2,1024]{2,1,0:T(2,128)} %redatum.1) | data formatting | bytes 1048576

commit v3 on v2

--- a/solution.py
+++ b/solution.py
@@ -17,6 +17,7 @@
 NN = (((1,), (0,)), ((), ()))
 TN = (((0,), (0,)), ((), ()))
 ACROSS = 4
+STRIDE = 2
 
 
 def dot(a, b, dims):
@@ -80,6 +81,7 @@
     ring_recv,
     y_send,
     y_recv,
+    first_sem,
     load_sem,
     x_sem,
     y_sem,
@@ -102,7 +104,7 @@
     z = r // 2
     c = r % 2
     partner = r + 1 - 2 * c
-    mates = [[lax.rem(r + nr - 2 * hops, nr), lax.rem(r + 2 * hops, nr)] for hops in (1, 2)]
+    mates = [[lax.rem(r + nr - 2 * hops, nr), lax.rem(r + 2 * hops, nr)] for hops in range(1, STRIDE + 1)]
     peers = far_first(nf)
 
     def peer(offset):
@@ -110,29 +112,29 @@
         columns = nf // ACROSS
         return lax.rem(f // columns + across, ACROSS) * columns + lax.rem(f + along, columns)
 
+    barrier = pltpu.get_barrier_semaphore()
+    for offset in peers:
+        pl.semaphore_signal(barrier, inc=1, device_id=(peer(offset), r), device_id_type=MESH)
+    for other in sum(mates[::-1], []) + [partner]:
+        pl.semaphore_signal(barrier, inc=1, device_id=(f, other), device_id_type=MESH)
+
+    parts = 4
+    deep = table.shape[1] // parts
+    first = []
+    for k in range(parts):
+        at = pl.ds(k * deep, deep)
+        for n, (far, near) in enumerate(((traces_hbm, traces), (table_hbm, table))):
+            first.append(pltpu.make_async_copy(far.at[:, at], near.at[:, at], first_sem.at[2 * k + n]))
+    for load in first:
+        load.start()
     loads = [
-        pltpu.make_async_copy(traces_hbm, traces, load_sem.at[0]),
-        pltpu.make_async_copy(table_hbm, table, load_sem.at[1]),
-        pltpu.make_async_copy(v_hbm, v_raw, load_sem.at[2]),
-        pltpu.make_async_copy(order_hbm, order, load_sem.at[3]),
+        pltpu.make_async_copy(v_hbm, v_raw, load_sem.at[0]),
+        pltpu.make_async_copy(order_hbm, order, load_sem.at[1]),
     ]
     for s in range(slots):
         loads.append(
-            pltpu.make_async_copy(u_hbm.at[s], u_all.at[:, pl.ds(s * cols, cols)], load_sem.at[4 + s])
+            pltpu.make_async_copy(u_hbm.at[s], u_all.at[:, pl.ds(s * cols, cols)], load_sem.at[2 + s])
         )
-    for load in loads:
-        load.start()
-
-    barrier = pltpu.get_barrier_semaphore()
-
-    def greet(i, carry):
-        p = lax.rem(f + i, nf)
-        pl.semaphore_signal(barrier, inc=1, device_id=(p, r), device_id_type=MESH)
-        return carry
-
-    lax.fori_loop(1, nf, greet, 0)
-    for other in [partner] + mates[0] + mates[1]:
-        pl.semaphore_signal(barrier, inc=1, device_id=(f, other), device_id_type=MESH)
 
     n2 = 2 * bins
     row = lax.broadcasted_iota(jnp.int32, (n2, bins), 0)
@@ -145,9 +147,15 @@
     lanes = lax.broadcasted_iota(jnp.int32, (n2, n2), 1).astype(F32)
     permute = jnp.where(lanes == want, 1.0, 0.0).astype(BF16)
 
-    loads[0].wait()
-    loads[1].wait()
-    spectra = dot(table[...], traces[...], NT) * (1.0 / math.sqrt(table.shape[1]))
+    spectra = jnp.zeros((n2, traces.shape[0]), F32)
+    for k in range(parts):
+        first[2 * k].wait()
+        first[2 * k + 1].wait()
+        at = slice(k * deep, (k + 1) * deep)
+        spectra = spectra + dot(table[:, at], traces[:, at], NT)
+    for load in loads:
+        load.start()
+    spectra = spectra * (1.0 / math.sqrt(table.shape[1]))
     spectra = dot(permute, spectra.astype(BF16), NN)
     groups = [spectra[:, k * rows : (k + 1) * rows].reshape(nf, 2 * slots, rows) for k in range(2)]
     block = 4 * slots
@@ -155,7 +163,7 @@
     mine = pl.ds(pl.multiple_of(f * block, block), block)
     x_recv[mine, :] = x_send[mine, :]
 
-    pl.semaphore_wait(barrier, nf + 4)
+    pl.semaphore_wait(barrier, nf + 2 * STRIDE)
 
     for offset in peers:
         p = peer(offset)
@@ -168,23 +176,27 @@
             device_id_type=MESH,
         ).start()
 
-    loads[2].wait()
+    loads[0].wait()
     lane_v = lax.broadcasted_iota(jnp.int32, (rows, cols), 1)
     lane_k = lane_v % rank_cap
     upper = lane_v < rank_cap
 
     for s in range(slots):
 
-        def prepare(i, carry, s=s):
-            v = jnp.where(lane_k < rank_ref[s, i], v_raw[s, i].astype(F32), 0.0)
-            turned = pltpu.roll(v, rank_cap, 1)
-            v_both[s, i, :rows, :] = v.astype(BF16)
-            v_both[s, i, rows:, :] = jnp.where(upper, turned, -turned).astype(BF16)
+        def prepare(g, carry, s=s):
+            down = lax.rem(z + steps + g, nz)
+            up = lax.rem(z + steps + nz - g + steps * ((steps - g) // steps), nz)
+            for h, i in enumerate((down, up)):
+                v = jnp.where(lane_k < rank_ref[s, i], v_raw[s, i].astype(F32), 0.0)
+                turned = pltpu.roll(v, rank_cap, 1)
+                at = slice(h * cols, (h + 1) * cols)
+                v_both[s, g, :rows, at] = v.astype(BF16)
+                v_both[s, g, rows:, at] = jnp.where(upper, turned, -turned).astype(BF16)
             return carry
 
-        lax.fori_loop(0, tiles, prepare, 0)
+        lax.fori_loop(0, steps, prepare, 0)
     slot_table[...] = dot(permute, table[...], NN).astype(BF16)
-    for load in loads[3:]:
+    for load in loads[1:]:
         load.wait()
 
     all_x = pltpu.make_async_remote_copy(
@@ -223,18 +235,26 @@
             device_id_type=MESH,
         )
 
-    def compute(n):
-        i = tile_at(n)
-        keep = pl.ds(pl.multiple_of(i * rows + c * half, half), half)
-        give = pl.ds(pl.multiple_of(i * rows + (1 - c) * half, half), half)
+    def compute(*some):
         for s in range(slots):
-            w = dot(left[s], v_both[s, i], NN).astype(BF16)
             at = slice(s * cols, (s + 1) * cols)
-            u = jnp.concatenate([u_all[keep, at], u_all[give, at]], axis=0)
-            y = dot(u, w, NT)
-            y_own[n, :, at] = y[:half]
-            pair_send[n, :, at] = y[half:].astype(BF16)
-        pair_copy(n).start()
+            group = (some[0] + 1) // 2 % steps
+            if len(some) == 2:
+                both = dot(left[s], v_both[s, group], NN).astype(BF16)
+                weights = [both[:, :cols], both[:, cols:]]
+            else:
+                column = cols if some[0] else 0
+                weights = [dot(left[s], v_both[s, group, :, column : column + cols], NN).astype(BF16)]
+            for n, w in zip(some, weights):
+                i = tile_at(n)
+                keep = pl.ds(pl.multiple_of(i * rows + c * half, half), half)
+                give = pl.ds(pl.multiple_of(i * rows + (1 - c) * half, half), half)
+                u = jnp.concatenate([u_all[keep, at], u_all[give, at]], axis=0)
+                y = dot(u, w, NT)
+                y_own[n, :, at] = y[:half]
+                pair_send[n, :, at] = y[half:].astype(BF16)
+        for n in some:
+            pair_copy(n).start()
 
     def ring_copy(way, m, p):
         return pltpu.make_async_remote_copy(
@@ -242,7 +262,7 @@
             dst_ref=ring_recv.at[way, m, p],
             send_sem=ring_send_sem.at[way, m, p],
             recv_sem=ring_recv_sem.at[way, m, p],
-            device_id=(f, mates[1 - m % 2][way]),
+            device_id=(f, mates[(steps - m - 1) % STRIDE][way]),
             device_id_type=MESH,
         )
 
@@ -250,6 +270,9 @@
         if m:
             return range(pieces)
         return range(pieces // 2, pieces) if way else range(pieces // 2)
+
+    def adds(m):
+        return m > 0 and (steps - m) % STRIDE == 0
 
     def own_part(n, p):
         at = slice(p * width, (p + 1) * width)
@@ -267,37 +290,31 @@
                 if p not in sent(way, m):
                     continue
                 total = own_part(0 if m == 0 else 2 * m - 1 + way, p)
-                if m and m % 2 == 0:
-                    for before in (m - 2, m - 1):
+                if adds(m):
+                    for before in range(m - STRIDE, m):
                         if p in sent(way, before):
                             total = total + arrived(way, before, p)
                 ring_send[way, m, p] = total.astype(BF16)
                 ring_copy(way, m, p).start()
 
     compute(0)
-    compute(1)
-    compute(2)
-    ring_stage(0)
-    ring_stage(1)
-    compute(3)
-    compute(4)
-    for m in range(2, steps, 2):
-        compute(2 * m + 1)
-        compute(2 * m + 2)
-        ring_stage(m + 1)
-        if m + 2 < steps:
-            compute(2 * m + 3)
-            compute(2 * m + 4)
+    for m in range(1, steps + 1):
+        if m < steps:
+            compute(2 * m - 1, 2 * m)
         else:
             compute(nz - 1)
-        ring_stage(m)
+        if not adds(m - 1):
+            ring_stage(m - 1)
+    for m in range(steps):
+        if adds(m):
+            ring_stage(m)
     n = nz - 1
     pair_copy(n).wait_recv()
     sums = []
     for p in range(pieces):
         total = own_part(n, p)
         for way in range(2):
-            for m in (steps - 2, steps - 1):
+            for m in range(steps - STRIDE, steps):
                 total = total + arrived(way, m, p)
         sums.append(total)
     response = jnp.concatenate(sums, axis=1)
@@ -369,7 +386,7 @@
         scratch_shapes=[
             pltpu.VMEM((local_shots * rows, moments), BF16),
             pltpu.VMEM((slots, tiles, rows, cols), BF16),
-            pltpu.VMEM((slots, tiles, 2 * rows, cols), BF16),
+            pltpu.VMEM((slots, steps, 2 * rows, 2 * cols), BF16),
             pltpu.VMEM((sources, wide), BF16),
             pltpu.VMEM((2 * bins, moments), BF16),
             pltpu.VMEM((nf * 2 * slots, wide), BF16),
@@ -385,7 +402,8 @@
             pltpu.VMEM((2, steps, pieces, half, wide // pieces), BF16),
             pltpu.VMEM((nf * 2 * slots, 2 * half), F32),
             pltpu.VMEM((nf * 2 * slots, 2 * half), F32),
-            pltpu.SemaphoreType.DMA((4 + slots,)),
+            pltpu.SemaphoreType.DMA((8,)),
+            pltpu.SemaphoreType.DMA((2 + slots,)),
             pltpu.SemaphoreType.DMA((2,)),
             pltpu.SemaphoreType.DMA((2,)),
             pltpu.SemaphoreType.DMA((nz,)),

time: 53.3 us -> 52.7 us (0.989)
  no operation moved by 1% of the time
where the time goes in v3:
time: 52.7 us; the launch traced here: 52.5 us
  Pallas kernels  50.6 us (96%)
  local copies, waits for them, and re-layouts  1.87 us (4%)
    pallas_call x1, Pallas kernels, on_device(): pl.pallas_call(functools.partial(kernel, nf, nr, pieces), out_shape=jax.S...  50.6 us
    unnamed x1, local copies, waits for them, and re-layouts  1.87 us

profile of v3, /device:TPU:8, one launch (start us, length us, event | category | flops | bytes accessed | tf_op | source)
XLA Modules:
  0.0 52.5 jit_solution(13914140114917969170)
XLA Ops:
  0.0 50.6 %redatum.1 = f32[64,2,1024]{2,1,0:T(2,128)} custom-call(bf16[256,1024]{1,0:T(8,128)(2,1)} %bitcast.7, bf16[4,12,128,128]{3,2,1,0:T(8,128)(2,1)} %bitcast.5, bf16[4,1536,128]{2,1,0:T(8,128)(2,1)} %bitcast.6, bf16[256,1024]{1,0:T(8,128)(2,1)} %constant.4.clone.table_hbm, bf16[256,512]{1,0:T(8,128)(2,1)} %constant.5.clone.order_hbm, s32[1,128]{1,0:T(1,128)} %bitcast.9, ...), custom_call_target="tpu_custom_call" | custom-call | tf_op jit(solution)/shard_map/redatum/pallas_call | solution.py:381
  50.6 1.9 %copy.9 = f32[64,2,1024]{2,1,0:T(2,128)} copy(f32[64,2,1024]{2,1,0:T(2,128)} %redatum.1) | data formatting | bytes 1048576
